TPU v7x, 32 devices: a whole 2x2x4 slice. The times are simulated.
32 devices in a mesh: batch: 4 (over x, core), patch: 8 (over z, y).
Axes of the slice: x: 2, y: 2, z: 4, core: 2. Of those that a mesh axis runs over, the one named last changes fastest.
Arguments:
- features: bfloat16 [24, 512, 1280], P('patch', 'batch'), parts along dimension 1, may hold values from -80 to 80
- stale_kv: bfloat16 [8, 3072, 640], P('batch', 'patch'), parts along dimension 0, may hold values from -260 to 260
- timestep: int32 [4], P('batch'), parts along dimension 0, may hold values from 0 to 999
- time_w: bfloat16 [320, 640], replicated, may hold values from -0.3125 to 0.3125
- gain_one: float32 [1280], replicated, may hold values from 0.5 to 1.5
- conv_w: bfloat16 [3, 3, 1280, 640], replicated, may hold values from -0.0546875 to 0.0546875
- shortcut_w: bfloat16 [1280, 640], replicated, may hold values from -0.078125 to 0.078125
- gain_two: float32 [640], replicated, may hold values from 0.5 to 1.5
- query_w: bfloat16 [640, 640], replicated, may hold values from -0.25 to 0.25
- key_w: bfloat16 [640, 640], replicated, may hold values from -0.5 to 0.5
- value_w: bfloat16 [640, 640], replicated, may hold values from -1 to 1
- out_w: bfloat16 [640, 640], replicated, may hold values from -0.25 to 0.25
Outputs:
- mixed_out: bfloat16 [24, 512, 640], P('patch', 'batch'), parts along dimension 1
There are 4 independent parts, one for each index of `batch`. A program takes and returns all parts, laid end to end along the dimension named above; an argument that names none is the same for every part. Nothing has to cross between parts.
All inputs are finite; a program needn't handle non-finite values.
Results may differ from a plain program's by a relative error of at most 0.014.
Values may be sent and summed in bfloat16 or wider, within the bound.
A program may use at most 192 MiB of HBM per device.

v0:
```python
import math

import jax
import jax.numpy as jnp
from jax import lax
from jax.sharding import PartitionSpec as P

HEAD_DIM = 64
GROUPS = 32
FREQ = 320


NEGATIVE = -1e30


def padded(cells, sides, width):
    for axis, dim in sides:
        count = lax.axis_size(axis)
        ends = count - 1
        head = lax.slice_in_dim(cells, 0, width, axis=dim)
        tail = lax.slice_in_dim(cells, cells.shape[dim] - width, cells.shape[dim], axis=dim)
        cells = jnp.concatenate(
            [
                lax.ppermute(tail, axis, [(i, (i + 1) % count) for i in range(ends)]),
                cells,
                lax.ppermute(head, axis, [((i + 1) % count, i) for i in range(ends)]),
            ],
            axis=dim,
        )
    return cells


def normalize(values, gain, eps):
    rows, cols, width = values.shape
    grouped = values.reshape(rows * cols, GROUPS, width // GROUPS)
    count = lax.axis_size("patch") * rows * cols * (width // GROUPS)
    first, second = lax.psum(
        (jnp.sum(grouped, axis=(0, 2)), jnp.sum(grouped * grouped, axis=(0, 2))), "patch"
    )
    center = first / count
    spread = second / count - center * center
    scaled = (grouped - center[None, :, None]) * lax.rsqrt(spread + eps)[None, :, None]
    return scaled.reshape(rows, cols, width) * gain


def block_partial(queries, keys, values):
    scores = jnp.einsum("qhd,khd->hqk", queries, keys, preferred_element_type=jnp.float32) * 0.125
    top = jnp.max(scores, axis=2)
    expo = jnp.exp(scores - top[:, :, None])
    total = jnp.sum(expo, axis=2)
    summed = jnp.einsum(
        "hqk,khd->hqd", expo.astype(jnp.bfloat16), values, preferred_element_type=jnp.float32
    )
    partial_value = (summed / total[:, :, None]).astype(jnp.bfloat16)
    return (partial_value, top + jnp.log(total))


def merge_block(carry, partial_value, lse, keep):
    best, weight_sum, accum = carry
    usable = jnp.where(keep, lse, NEGATIVE)
    top = jnp.maximum(best, usable)
    old_factor = jnp.exp(best - top)
    new_factor = jnp.exp(usable - top)
    weight_sum = weight_sum * old_factor + new_factor
    accum = accum * old_factor[:, :, None] + new_factor[:, :, None] * partial_value.astype(
        jnp.float32
    )
    return (top, weight_sum, accum)


def on_device(
    features,
    stale_kv,
    timestep,
    time_w,
    gain_one,
    conv_w,
    shortcut_w,
    gain_two,
    query_w,
    key_w,
    value_w,
    out_w,
):
    rows, cols, width_in = features.shape
    width_out = shortcut_w.shape[1]
    heads = width_out // HEAD_DIM
    block = rows * cols
    act = jax.nn.silu(normalize(features.astype(jnp.float32), gain_one, 1e-05)).astype(jnp.bfloat16)
    edged = padded(act, (("patch", 0),), 1)
    edged = jnp.pad(edged, ((0, 0), (1, 1), (0, 0)))
    conv = jnp.zeros((block, width_out), jnp.float32)
    for row_off in range(3):
        for col_off in range(3):
            window = edged[row_off : row_off + rows, col_off : col_off + cols].reshape(
                block, width_in
            )
            conv = conv + jnp.dot(
                window, conv_w[row_off, col_off], preferred_element_type=jnp.float32
            )
    half = FREQ // 2
    freqs = jnp.exp(-math.log(10000.0) * jnp.arange(half, dtype=jnp.float32) / half)
    angles = timestep.astype(jnp.float32)[0] * freqs
    embed = jnp.concatenate([jnp.cos(angles), jnp.sin(angles)]).astype(jnp.bfloat16)
    shift = jnp.dot(embed[None, :], time_w, preferred_element_type=jnp.float32)
    mixed = (
        jnp.dot(features.reshape(block, width_in), shortcut_w, preferred_element_type=jnp.float32)
        + conv
        + shift
    )
    normed = (
        normalize(mixed.reshape(rows, cols, width_out), gain_two, 1e-06)
        .astype(jnp.bfloat16)
        .reshape(block, width_out)
    )
    queries = (
        jnp.dot(normed, query_w, preferred_element_type=jnp.float32)
        .astype(jnp.bfloat16)
        .reshape(block, heads, HEAD_DIM)
    )
    fresh_keys = (
        jnp.dot(normed, key_w, preferred_element_type=jnp.float32)
        .astype(jnp.bfloat16)
        .reshape(block, heads, HEAD_DIM)
    )
    fresh_values = (
        jnp.dot(normed, value_w, preferred_element_type=jnp.float32)
        .astype(jnp.bfloat16)
        .reshape(block, heads, HEAD_DIM)
    )
    own_partial, own_lse = block_partial(queries, fresh_keys, fresh_values)
    local = (own_lse, jnp.ones((heads, block), jnp.float32), own_partial.astype(jnp.float32))
    own_index = lax.axis_index("patch")
    own_start = own_index * block
    carry = local
    piece = lax.all_gather(stale_kv, "patch", axis=1, tiled=True)
    length = piece.shape[1]
    pieces = length // block
    key_rows = piece[0].reshape(pieces, block, heads, HEAD_DIM)
    value_rows = piece[1].reshape(pieces, block, heads, HEAD_DIM)

    def step(inner, item):
        index, keys, values = item
        keep = index * block != own_start
        partial_value, lse = block_partial(queries, keys, values)
        return (merge_block(inner, partial_value, lse, keep), None)

    carry, unused = lax.scan(
        step, carry, (jnp.arange(pieces, dtype=jnp.int32), key_rows, value_rows)
    )
    best, total, weighted = carry
    result = weighted / total[:, :, None]
    attended = jnp.transpose(result, (1, 0, 2)).reshape(block, width_out).astype(jnp.bfloat16)
    output = mixed + jnp.dot(attended, out_w, preferred_element_type=jnp.float32)
    return output.astype(jnp.bfloat16).reshape(rows, cols, width_out)


def solution(mesh):
    return jax.shard_map(
        on_device,
        mesh=mesh,
        in_specs=(
            P("patch", "batch", None),
            P("batch", "patch", None),
            P("batch"),
            P(),
            P(),
            P(),
            P(),
            P(),
            P(),
            P(),
            P(),
            P(),
        ),
        out_specs=P("patch", "batch", None),
        check_vma=False,
    )
```

profile of v0, /device:TPU:0, one launch (start us, length us, event | category | flops | bytes accessed | tf_op | source)
XLA Modules:
  0.0 276.1 jit_solution(6806537783885888574)
XLA Ops:
  9.1 23.5 %all-reduce.2 = (f32[32]{0:T(128)S(1)}, f32[32]{0:T(128)S(1)}) all-reduce(f32[32]{0:T(128)S(1)} %reduce_sum.73, f32[32]{0:T(128)S(1)} %reduce_sum.67), channel_id=1, replica_groups=mesh['batch'=4,'patch'=8] {'patch'}, use_global_device_ids=true, to_apply=%region_5.6 | all-reduce | flops 64 | bytes 512 | tf_op jit(solution)/shard_map/psum | solution.py:37
  39.1 3.4 %fusion.61 = f32[384,640]{1,0:T(8,128)} fusion(bf16[384,1280]{1,0:T(8,128)(2,1)S(1)} %bitcast.153, bf16[3,3,1280,640]{3,2,1,0:T(8,128)(2,1)} %param.19), kind=kOutput, calls=%fused_computation.62 | convolution fusion | flops 629145600 | bytes 3604480 | tf_op jit(solution)/shard_map/dot_general | solution.py:98
  43.7 2.3 fusion.126
  47.4 3.0 %fusion.63 = f32[384,640]{1,0:T(8,128)S(1)} fusion(bf16[384,1280]{1,0:T(8,128)(2,1)S(1)} %bitcast.164, bf16[3,3,1280,640]{3,2,1,0:T(8,128)(2,1)} %param.19), kind=kOutput, calls=%fused_computation.64 | convolution fusion | flops 629145600 | bytes 3604480 | tf_op jit(solution)/shard_map/dot_general | solution.py:98
  58.0 34.6 %all-reduce.1 = (f32[32]{0:T(128)S(1)}, f32[32]{0:T(128)S(1)}) all-reduce(f32[32]{0:T(128)S(1)} %reduce_sum.93, f32[32]{0:T(128)S(1)} %reduce_sum.90), channel_id=1, replica_groups=mesh['batch'=4,'patch'=8] {'patch'}, use_global_device_ids=true, to_apply=%region_11.12 | all-reduce | flops 64 | bytes 512 | tf_op jit(solution)/shard_map/psum | solution.py:37
  97.2 2.5 convolution_convert_fusion
  105.1 33.2 %all-gather.2.cloned.1.call-done = bf16[2,3072,640]{2,1,0:T(8,128)(2,1)} async-done(((bf16[2,384,640]{2,1,0:T(8,128)(2,1)}), bf16[2,3072,640]{2,1,0:T(8,128)(2,1)}) %all-gather.2.cloned.1.call-update) | async-done | bytes 7864336 | tf_op jit(solution)/shard_map/all_gather | solution.py:136
  138.3 5.5 %fusion.123 = (bf16[1,3072,640]{2,1,0:T(8,128)(2,1)}, bf16[1,3072,640]{2,1,0:T(8,128)(2,1)}) fusion(bf16[2,3072,640]{2,1,0:T(8,128)(2,1)} %all-gather.2.cloned.1.call-done), kind=kLoop, calls=%fused_computation.116 | loop fusion | bytes 15728640 | tf_op jit(solution)/shard_map/slice | solution.py:140
  143.9 6.3 %copy.33 = bf16[1,3072,640]{1,2,0:T(8,128)(2,1)} copy(bf16[1,3072,640]{2,1,0:T(8,128)(2,1)} %get-tuple-element.145) | data formatting | bytes 7864320 | tf_op jit(solution)/shard_map/slice | solution.py:139
  150.1 3.1 %copy.39 = bf16[80,8,8,384]{3,2,1,0:T(8,128)(2,1)S(1)} copy(bf16[80,8,8,384]{3,1,2,0:T(8,128)(2,1)} %bitcast.149) | data formatting | bytes 7864320
  153.2 2.7 copy.35
  155.9 6.4 %copy.34 = bf16[1,3072,640]{1,2,0:T(8,128)(2,1)} copy(bf16[1,3072,640]{2,1,0:T(8,128)(2,1)} %get-tuple-element.144) | data formatting | bytes 7864320 | tf_op jit(solution)/shard_map/slice | solution.py:140
  162.2 3.1 %copy.40 = bf16[80,8,8,384]{3,2,1,0:T(8,128)(2,1)S(1)} copy(bf16[80,8,8,384]{3,1,2,0:T(8,128)(2,1)} %bitcast.151) | data formatting | bytes 7864320
  165.3 2.7 copy.36
  168.0 97.2 %while.15 = (s32[]{:T(128)}, f32[10,384]{1,0:T(8,128)S(1)}, f32[10,384]{1,0:T(8,128)S(1)}, f32[10,384,64]{1,2,0:T(8,128)}, s32[8]{0:T(128)S(1)}, /*index=5*/s32[...) while((s32[]{:T(128)}, f32[10,384]{1,0:T(8,128)S(1)}, ...), condition=%wide.region_17.18_spmd.clone, body=%wide.region_14.17_spmd.clone.sunk | while | flops 390781440 | bytes 44959932 | solution.py:148
  170.1 2.6 copy-done.2
  174.9 5.3 %fusion.163 = f32[10,384,64]{1,2,0:T(8,128)} fusion(f32[10,384,384]{2,1,0:T(8,128)} %copy-done.2, f32[10,384]{1,0:T(8,128)S(1)} %get-tuple-element.226, f32[10,384,64]{1,2,0:T(8,128)} %get-tuple-element.247, f32[10,384]{1,0:T(8,128)S(1)} %fusion.161, bf16[8,384,10,64]{1,3,2,0:T(8,128)(2,1)} %get-tuple-element.264, s32[]{:T(128)} %get-tuple-element.244, ...), kind=kOutput, calls=%fused_computation.12.clone.1 | convolution fusion | flops 194641920 | bytes 8417792 | tf_op jit(solution)/shard_map/while/body/eval_jaxpr/hqk,khd->hqd/dot_general | solution.py:51
  182.2 2.6 copy-done.2
  187.1 5.3 %fusion.163 = f32[10,384,64]{1,2,0:T(8,128)} fusion(f32[10,384,384]{2,1,0:T(8,128)} %copy-done.2, f32[10,384]{1,0:T(8,128)S(1)} %get-tuple-element.226, f32[10,384,64]{1,2,0:T(8,128)} %get-tuple-element.247, f32[10,384]{1,0:T(8,128)S(1)} %fusion.161, bf16[8,384,10,64]{1,3,2,0:T(8,128)(2,1)} %get-tuple-element.264, s32[]{:T(128)} %get-tuple-element.244, ...), kind=kOutput, calls=%fused_computation.12.clone.1 | convolution fusion | flops 194641920 | bytes 8417792 | tf_op jit(solution)/shard_map/while/body/eval_jaxpr/hqk,khd->hqd/dot_general | solution.py:51
  194.4 2.6 copy-done.2
  199.2 5.3 %fusion.163 = f32[10,384,64]{1,2,0:T(8,128)} fusion(f32[10,384,384]{2,1,0:T(8,128)} %copy-done.2, f32[10,384]{1,0:T(8,128)S(1)} %get-tuple-element.226, f32[10,384,64]{1,2,0:T(8,128)} %get-tuple-element.247, f32[10,384]{1,0:T(8,128)S(1)} %fusion.161, bf16[8,384,10,64]{1,3,2,0:T(8,128)(2,1)} %get-tuple-element.264, s32[]{:T(128)} %get-tuple-element.244, ...), kind=kOutput, calls=%fused_computation.12.clone.1 | convolution fusion | flops 194641920 | bytes 8417792 | tf_op jit(solution)/shard_map/while/body/eval_jaxpr/hqk,khd->hqd/dot_general | solution.py:51
  206.5 2.6 copy-done.2
  211.4 5.3 %fusion.163 = f32[10,384,64]{1,2,0:T(8,128)} fusion(f32[10,384,384]{2,1,0:T(8,128)} %copy-done.2, f32[10,384]{1,0:T(8,128)S(1)} %get-tuple-element.226, f32[10,384,64]{1,2,0:T(8,128)} %get-tuple-element.247, f32[10,384]{1,0:T(8,128)S(1)} %fusion.161, bf16[8,384,10,64]{1,3,2,0:T(8,128)(2,1)} %get-tuple-element.264, s32[]{:T(128)} %get-tuple-element.244, ...), kind=kOutput, calls=%fused_computation.12.clone.1 | convolution fusion | flops 194641920 | bytes 8417792 | tf_op jit(solution)/shard_map/while/body/eval_jaxpr/hqk,khd->hqd/dot_general | solution.py:51
  218.7 2.6 copy-done.2
  223.5 5.3 %fusion.163 = f32[10,384,64]{1,2,0:T(8,128)} fusion(f32[10,384,384]{2,1,0:T(8,128)} %copy-done.2, f32[10,384]{1,0:T(8,128)S(1)} %get-tuple-element.226, f32[10,384,64]{1,2,0:T(8,128)} %get-tuple-element.247, f32[10,384]{1,0:T(8,128)S(1)} %fusion.161, bf16[8,384,10,64]{1,3,2,0:T(8,128)(2,1)} %get-tuple-element.264, s32[]{:T(128)} %get-tuple-element.244, ...), kind=kOutput, calls=%fused_computation.12.clone.1 | convolution fusion | flops 194641920 | bytes 8417792 | tf_op jit(solution)/shard_map/while/body/eval_jaxpr/hqk,khd->hqd/dot_general | solution.py:51
  230.8 2.6 copy-done.2
  235.7 5.3 %fusion.163 = f32[10,384,64]{1,2,0:T(8,128)} fusion(f32[10,384,384]{2,1,0:T(8,128)} %copy-done.2, f32[10,384]{1,0:T(8,128)S(1)} %get-tuple-element.226, f32[10,384,64]{1,2,0:T(8,128)} %get-tuple-element.247, f32[10,384]{1,0:T(8,128)S(1)} %fusion.161, bf16[8,384,10,64]{1,3,2,0:T(8,128)(2,1)} %get-tuple-element.264, s32[]{:T(128)} %get-tuple-element.244, ...), kind=kOutput, calls=%fused_computation.12.clone.1 | convolution fusion | flops 194641920 | bytes 8417792 | tf_op jit(solution)/shard_map/while/body/eval_jaxpr/hqk,khd->hqd/dot_general | solution.py:51
  243.0 2.6 copy-done.2
  247.8 5.3 %fusion.163 = f32[10,384,64]{1,2,0:T(8,128)} fusion(f32[10,384,384]{2,1,0:T(8,128)} %copy-done.2, f32[10,384]{1,0:T(8,128)S(1)} %get-tuple-element.226, f32[10,384,64]{1,2,0:T(8,128)} %get-tuple-element.247, f32[10,384]{1,0:T(8,128)S(1)} %fusion.161, bf16[8,384,10,64]{1,3,2,0:T(8,128)(2,1)} %get-tuple-element.264, s32[]{:T(128)} %get-tuple-element.244, ...), kind=kOutput, calls=%fused_computation.12.clone.1 | convolution fusion | flops 194641920 | bytes 8417792 | tf_op jit(solution)/shard_map/while/body/eval_jaxpr/hqk,khd->hqd/dot_general | solution.py:51
  255.1 2.6 copy-done.2
  260.0 5.3 %fusion.163 = f32[10,384,64]{1,2,0:T(8,128)} fusion(f32[10,384,384]{2,1,0:T(8,128)} %copy-done.2, f32[10,384]{1,0:T(8,128)S(1)} %get-tuple-element.226, f32[10,384,64]{1,2,0:T(8,128)} %get-tuple-element.247, f32[10,384]{1,0:T(8,128)S(1)} %fusion.161, bf16[8,384,10,64]{1,3,2,0:T(8,128)(2,1)} %get-tuple-element.264, s32[]{:T(128)} %get-tuple-element.244, ...), kind=kOutput, calls=%fused_computation.12.clone.1 | convolution fusion | flops 194641920 | bytes 8417792 | tf_op jit(solution)/shard_map/while/body/eval_jaxpr/hqk,khd->hqd/dot_general | solution.py:51
  266.7 2.6 fusion.110
  (111 shorter events, 58.6 us)
Async XLA Ops:
  6.5 37.1 %copy-start = (bf16[1280,640]{1,0:T(8,128)(2,1)S(1)}, bf16[1280,640]{1,0:T(8,128)(2,1)}, u32[]{:S(2)}) copy-start(bf16[1280,640]{1,0:T(8,128)(2,1)} %param.20) | copy-start | bytes 4915204
  6.5 131.8 %all-gather.2.cloned.1.call-start = ((), (), s32[]{:S(2)}) async-start(), calls=%async_computation | async-start | bytes 8847360 | tf_op jit(solution)/shard_map/all_gather | solution.py:136
  35.7 10.3 %collective-permute-start = (bf16[1,128,1280]{2,1,0:T(8,128)(2,1)}, bf16[1,128,1280]{2,1,0:T(8,128)(2,1)S(1)}, u32[]{:S(2)}, u32[]{:S(2)}) collective-permute-start(bf16[1,128,1280]{2,1,0:T(8,128)(2,1)} %get-tuple-element.154), channel_id=1, source_target_pairs={{0,1},{1,2},{2,3},{3,4},{4,5},{5,6},{6,7},{8,9},{9,10},{10,11},{11... | collective-permute-start | bytes 983048 | tf_op jit(solution)/shard_map/ppermute | solution.py:24
  37.0 9.2 %collective-permute-start.1 = (bf16[1,128,1280]{2,1,0:T(8,128)(2,1)}, bf16[1,128,1280]{2,1,0:T(8,128)(2,1)S(1)}, u32[]{:S(2)}, u32[]{:S(2)}) collective-permute-start(bf16[1,128,1280]{2,1,0:T(8,128)(2,1)} %get-tuple-element.155), channel_id=1, source_target_pairs={{1,0},{2,1},{3,2},{4,3},{5,4},{6,5},{7,6},{9,8},{10,9},{11,10},{12... | collective-permute-start | bytes 983048 | tf_op jit(solution)/shard_map/ppermute | solution.py:26
  43.7 6.7 %slice-start = ((s8[14745600]{0:T(1024)(128)(4,1)}), s8[4194304]{0:T(1024)(128)(4,1)S(1)}, s32[]{:S(2)}) async-start(s8[14745600]{0:T(1024)(128)(4,1)} %bitcast.165), calls=%async_computation.1 | async-start | bytes 8388608
  46.0 4.4 %slice-start.1 = ((s8[14745600]{0:T(1024)(128)(4,1)}), s8[4194304]{0:T(1024)(128)(4,1)S(1)}, s32[]{:S(2)}) async-start(s8[14745600]{0:T(1024)(128)(4,1)} %bitcast.165), calls=%async_computation.2 | async-start | bytes 8388608
  46.8 3.7 %slice-start.2 = ((s8[14745600]{0:T(1024)(128)(4,1)}), s8[4194304]{0:T(1024)(128)(4,1)S(1)}, s32[]{:S(2)}) async-start(s8[14745600]{0:T(1024)(128)(4,1)} %bitcast.165), calls=%async_computation.3 | async-start | bytes 8388608
  46.8 3.9 %slice-start.3 = ((s8[14745600]{0:T(1024)(128)(4,1)}), s8[2162688]{0:T(1024)(128)(4,1)S(1)}, s32[]{:S(2)}) async-start(s8[14745600]{0:T(1024)(128)(4,1)} %bitcast.165), calls=%async_computation.4 | async-start | bytes 4325376
  53.5 1.9 copy-start.3
  56.5 36.5 %copy-start.4 = (f32[640]{0:T(1024)S(1)}, f32[640]{0:T(1024)}, u32[]{:S(2)}) copy-start(f32[640]{0:T(1024)} %param.21) | copy-start | bytes 7684
  170.1 2.6 copy-start.2
  182.2 2.6 copy-start.2
  194.4 2.6 copy-start.2
  206.5 2.6 copy-start.2
  218.7 2.6 copy-start.2
  230.8 2.6 copy-start.2
  243.0 2.6 copy-start.2
  255.1 2.6 copy-start.2
  265.3 4.0 %copy-start.1 = (bf16[1280,640]{1,0:T(8,128)(2,1)S(1)}, bf16[1280,640]{1,0:T(8,128)(2,1)}, u32[]{:S(2)}) copy-start(bf16[1280,640]{1,0:T(8,128)(2,1)} %param.20) | copy-start | bytes 4915204
Sparse Core Ops, SparseCore 0:
  9.6 128.7 all-gather.1
where the time goes:
time: 277 us; the launch traced here: 276 us
  matrix products  86.6 us (31%)
  local copies, waits for them, and re-layouts  59.7 us (22%)
  blocking collectives  58.1 us (21%)
  waiting for transfers between devices  34 us (12%)
  other arithmetic  15.1 us (5%)
  between operations  14.4 us (5%)
  loops' own time  5.51 us (2%)
    psum x2, blocking collectives, normalize(): lax.psum((jnp.sum(grouped, axis=(0, 2)), jnp.sum(grouped * grouped, axis=...  58.1 us
    dot_general x9, matrix products, block_partial(): jnp.einsum('hqk,khd->hqd', expo.astype(jnp.bfloat16), values, preferred_e...  44.4 us
    all_gather x1, waiting for transfers between devices, on_device(): piece = lax.all_gather(stale_kv, 'patch', axis=1, tiled=True)  33.2 us
    while x16, local copies, waits for them, and re-layouts  20.6 us
    dot_general x9, matrix products, block_partial(): jnp.einsum('qhd,khd->hqk', queries, keys, preferred_element_type=jnp.floa...  17.1 us
    dot_general x9, matrix products, on_device(): jnp.dot(window, conv_w[row_off, col_off], preferred_element_type=jnp.floa...  13.1 us
    slice x2, local copies, waits for them, and re-layouts, on_device(): value_rows = piece[1].reshape(pieces, block, heads, HEAD_DIM)  11.9 us
    unnamed x20, local copies, waits for them, and re-layouts  11.8 us
  transfers between devices with their start and end apart: 3, of which 2 were waited for; matrix products, arithmetic and copies ran while one was open for 13% of the time, Pallas kernels for 0%

commit v1 on v0

v1 whole, which is shorter than its diff:
```python
import functools
import math

import jax
import jax.numpy as jnp
from jax import lax
from jax.experimental import pallas as pl
from jax.experimental.pallas import tpu as pltpu
from jax.sharding import PartitionSpec as P

HEAD_DIM = 64
GROUPS = 32
FREQ = 320
LANES = 128
F32 = jnp.float32
BF16 = jnp.bfloat16
EXP_SCALE = 0.125 * math.log2(math.e)
LN2 = math.log(2.0)
MESH = pl.DeviceIdType.MESH


def dot(a, b):
    return jnp.dot(a, b, preferred_element_type=F32)


def split_dot(a, b):
    high = a.astype(BF16)
    rest = a - high.astype(F32)
    mid = rest.astype(BF16)
    low = (rest - mid.astype(F32)).astype(BF16)
    return dot(high, b) + dot(mid, b) + dot(low, b)


def members(shape, chan_dim, size):
    chan = lax.broadcasted_iota(jnp.int32, shape, chan_dim)
    group = lax.broadcasted_iota(jnp.int32, shape, 1 - chan_dim) * size
    return jnp.where((chan >= group) & (chan < group + size), 1.0, 0.0).astype(BF16)


def two_rows(first, second):
    row = lax.broadcasted_iota(jnp.int32, (8, first.shape[1]), 0)
    return jnp.where(row == 0, first, jnp.where(row == 1, second, 0.0))


def group_stats(total, count, eps):
    width = total.shape[1]
    size = width // GROUPS
    grouped = split_dot(total, members((width, LANES), 0, size))
    center = grouped[0:1] / count
    spread = jnp.maximum(grouped[1:2] / count - center * center, 0.0)
    wide = split_dot(two_rows(center, lax.rsqrt(spread + eps)), members((LANES, width), 1, size))
    return wide[0:1], wide[1:2]


def half_mask(rows):
    return lax.broadcasted_iota(jnp.int32, (rows, LANES), 1) < HEAD_DIM


def scores_of(query, keys):
    return lax.dot_general(query, keys, (((1,), (1,)), ((), ())), preferred_element_type=F32)


def fused_kernel(
    size,
    kv_ref,
    feat_ref,
    embed_ref,
    time_ref,
    gain_one_ref,
    conv_ref,
    short_ref,
    gain_two_ref,
    qw_ref,
    kw_ref,
    vw_ref,
    ow_ref,
    out_ref,
    feat,
    convw,
    shortw,
    projw,
    act,
    parts,
    mixed,
    kvs,
    stat_out1,
    stat_in1,
    stat_out2,
    stat_in2,
    fresh,
    q_in,
    own_val,
    own_lse,
    acc,
    top,
    res,
    res_lse,
    res_in,
    lse_in,
    load_sem,
    conv_sem,
    kv_send,
    kv_recv,
    kv_own,
    stat_send,
    stat_recv,
    halo_send,
    halo_recv,
    q_send,
    q_recv,
    res_send,
    res_recv,
    lse_send,
    lse_recv,
):
    me = lax.axis_index("patch")
    block, width_in = feat.shape
    width = mixed.shape[1]
    pairs = width // LANES
    cols = (act.shape[0] - block) // 2

    loads = [
        pltpu.make_async_copy(feat_ref, feat, load_sem.at[0]),
        pltpu.make_async_copy(short_ref, shortw, load_sem.at[1]),
        pltpu.make_async_copy(qw_ref, projw.at[0], load_sem.at[2]),
        pltpu.make_async_copy(kw_ref, projw.at[1], load_sem.at[3]),
        pltpu.make_async_copy(vw_ref, projw.at[2], load_sem.at[4]),
        pltpu.make_async_copy(ow_ref, projw.at[3], load_sem.at[5]),
    ]
    conv_loads = [
        [
            pltpu.make_async_copy(conv_ref.at[dy, dx], convw.at[dy, dx], conv_sem.at[dy, dx])
            for dx in range(3)
        ]
        for dy in range(3)
    ]
    loads[0].start()
    loads[1].start()
    for dy in (1, 0, 2):
        for dx in range(3):
            conv_loads[dy][dx].start()
    for load in loads[2:]:
        load.start()

    barrier = pltpu.get_barrier_semaphore()

    def greet(step, unused):
        pl.semaphore_signal(
            barrier, inc=1, device_id={"patch": lax.rem(me + step, size)}, device_id_type=MESH
        )
        return unused

    lax.fori_loop(1, size, greet, 0)

    def first_pair(device):
        return lax.div(device * pairs, size)

    def last_pair(device):
        return lax.div(device * pairs + pairs - 1, size)

    def stale(pair):
        return kv_ref.at[:, :, pl.ds(pl.multiple_of(pair * LANES, LANES), LANES)]

    def place(slot, owner):
        return kvs.at[slot, :, pl.ds(pl.multiple_of(owner * block, block), block), :]

    def kv_copy(slot, pair, target, index):
        return pltpu.make_async_remote_copy(
            src_ref=stale(pair),
            dst_ref=place(slot, me),
            send_sem=kv_send.at[slot, target],
            recv_sem=kv_recv.at[slot, index],
            device_id={"patch": target},
            device_id_type=MESH,
        )

    my_first = first_pair(me)
    my_last = last_pair(me)
    own_copies = [
        pltpu.make_async_copy(stale(my_first), place(0, me), kv_own.at[0]),
        pltpu.make_async_copy(stale(my_last), place(1, me), kv_own.at[1]),
    ]
    own_copies[0].start()
    own_copies[1].start()

    loads[0].wait()

    def sum_rows(step, carry):
        first, second = carry
        x = feat[pl.ds(pl.multiple_of(step * 16, 16), 16), :].astype(F32)
        low, high = x[:8], x[8:]
        return first + (low + high), second + (low * low + high * high)

    zero = jnp.zeros((8, width_in), F32)
    first, second = lax.fori_loop(0, block // 16, sum_rows, (zero, zero))
    stat_out1[...] = two_rows(
        jnp.sum(first, axis=0, keepdims=True), jnp.sum(second, axis=0, keepdims=True)
    )
    pl.semaphore_wait(barrier, size - 1)

    def stat_copy(which, out, into, target, index):
        return pltpu.make_async_remote_copy(
            src_ref=out,
            dst_ref=into.at[me],
            send_sem=stat_send.at[which, target],
            recv_sem=stat_recv.at[which, index],
            device_id={"patch": target},
            device_id_type=MESH,
        )

    def stats_start(which, out, into):
        def send(step, unused):
            target = lax.rem(me + step, size)
            stat_copy(which, out, into, target, me).start()
            return unused

        lax.fori_loop(1, size, send, 0)

    def stats_finish(which, out, into):
        def receive(step, total):
            source = lax.rem(me + step, size)
            pltpu.make_async_remote_copy(
                src_ref=out,
                dst_ref=into.at[source],
                send_sem=stat_send.at[which, source],
                recv_sem=stat_recv.at[which, source],
                device_id={"patch": source},
                device_id_type=MESH,
            ).wait()
            return total + into[source]

        return lax.fori_loop(1, size, receive, out[...])

    stats_start(0, stat_out1, stat_in1)

    def send_kv(step, unused):
        target = lax.rem(me + step, size)
        kv_copy(0, first_pair(target), target, me).start()

        @pl.when(last_pair(target) != first_pair(target))
        def _():
            kv_copy(1, last_pair(target), target, me).start()

        return unused

    lax.fori_loop(1, size, send_kv, 0)

    loads[1].wait()
    mixed[...] = dot(feat[...], shortw[...]) + dot(embed_ref[...], time_ref[...])[0:1]

    total = stats_finish(0, stat_out1, stat_in1)
    count = float(size * block * (width_in // GROUPS))
    center, inverse = group_stats(total, count, 1e-05)
    scale = inverse * gain_one_ref[...]

    def activate(step, unused):
        x = feat[pl.ds(pl.multiple_of(step * 16, 16), 16), :].astype(F32)
        y = (x - center) * scale
        half = 0.5 * y
        z = half + half * jnp.tanh(half)
        act[pl.ds(pl.multiple_of(cols + step * 16, 16), 16), :] = z.astype(BF16)
        return unused

    lax.fori_loop(0, block // 16, activate, 0)

    top_row = act.at[pl.ds(cols, cols), :]
    bottom_row = act.at[pl.ds(block, cols), :]
    above = act.at[pl.ds(0, cols), :]
    below = act.at[pl.ds(block + cols, cols), :]
    up = pltpu.make_async_remote_copy(
        src_ref=top_row,
        dst_ref=below,
        send_sem=halo_send.at[0],
        recv_sem=halo_recv.at[0],
        device_id={"patch": lax.rem(me + size - 1, size)},
        device_id_type=MESH,
    )
    down = pltpu.make_async_remote_copy(
        src_ref=bottom_row,
        dst_ref=above,
        send_sem=halo_send.at[1],
        recv_sem=halo_recv.at[1],
        device_id={"patch": lax.rem(me + 1, size)},
        device_id_type=MESH,
    )

    @pl.when(me > 0)
    def _():
        up.start()

    @pl.when(me < size - 1)
    def _():
        down.start()

    @pl.when(me == 0)
    def _():
        above[...] = jnp.zeros((cols, width_in), BF16)

    @pl.when(me == size - 1)
    def _():
        below[...] = jnp.zeros((cols, width_in), BF16)

    for dx in range(3):
        conv_loads[1][dx].wait()

    def middle(dx, unused):
        parts[dx] = dot(act[pl.ds(cols, block), :], convw[1, dx])
        return unused

    lax.fori_loop(0, 3, middle, 0)

    for dy in (0, 2):
        for dx in range(3):
            conv_loads[dy][dx].wait()

    @pl.when(me > 0)
    def _():
        up.wait_send()
        down.wait_recv()

    @pl.when(me < size - 1)
    def _():
        down.wait_send()
        up.wait_recv()

    def outer(dx, unused):
        parts[dx] = (
            parts[dx]
            + dot(act[pl.ds(0, block), :], convw[0, dx])
            + dot(act[pl.ds(2 * cols, block), :], convw[2, dx])
        )
        return unused

    lax.fori_loop(0, 3, outer, 0)

    col = lax.rem(lax.broadcasted_iota(jnp.int32, (block, LANES), 0), cols)
    for pair in range(pairs):
        lanes = pl.ds(pair * LANES, LANES)
        left = jnp.where(col == 0, 0.0, pltpu.roll(parts[0, :, lanes], 1, 0))
        right = jnp.where(col == cols - 1, 0.0, pltpu.roll(parts[2, :, lanes], block - 1, 0))
        value = mixed[:, lanes] + (left + parts[1, :, lanes] + right)
        mixed[:, lanes] = value
        stat_out2[:, lanes] = two_rows(
            jnp.sum(value, axis=0, keepdims=True), jnp.sum(value * value, axis=0, keepdims=True)
        )
    stats_start(1, stat_out2, stat_in2)
    for load in loads[2:]:
        load.wait()
    total = stats_finish(1, stat_out2, stat_in2)
    count = float(size * block * (width // GROUPS))
    center, inverse = group_stats(total, count, 1e-06)
    normed = ((mixed[...] - center) * (inverse * gain_two_ref[...])).astype(BF16)

    def task_of(pair):
        task = pair * size + me
        return lax.div(task, pairs), lax.rem(task, pairs)

    def q_remote(pair, target, slot):
        return pltpu.make_async_remote_copy(
            src_ref=fresh.at[0, pair],
            dst_ref=q_in.at[slot],
            send_sem=q_send.at[pair],
            recv_sem=q_recv.at[slot],
            device_id={"patch": target},
            device_id_type=MESH,
        )

    queries = dot(normed, projw[0]).astype(BF16)
    for pair in range(pairs):
        fresh[0, pair] = queries[:, pair * LANES : (pair + 1) * LANES]
    for pair in range(pairs):
        target, slot = task_of(pair)

        @pl.when(target != me)
        def _():
            q_remote(pair, target, slot).start()

        @pl.when(target == me)
        def _():
            pltpu.make_async_copy(fresh.at[0, pair], q_in.at[slot], q_recv.at[slot]).start()

    for kind in (1, 2):
        value = dot(normed, projw[kind]).astype(BF16)
        for pair in range(pairs):
            fresh[kind, pair] = value[:, pair * LANES : (pair + 1) * LANES]

    left_half = half_mask(block)
    ones = jnp.ones((block, LANES), BF16)

    def heads_of(query):
        none = jnp.zeros_like(query)
        return jnp.where(left_half, query, none), jnp.where(left_half, none, query)

    def finish(pieces):
        values, lses = [], []
        for summed, height in pieces:
            weight = summed[:, LANES:]
            values.append(summed[:, :LANES] / weight)
            lses.append(height * 0.125 + jnp.log(weight))
        return jnp.where(left_half, *values), jnp.where(left_half, *lses)

    def own_attention(pair, unused):
        keys = fresh[1, pair]
        values = jnp.concatenate([fresh[2, pair], ones], axis=1)
        pieces = []
        for query in heads_of(fresh[0, pair]):
            scores = scores_of(query, keys)
            height = jnp.max(scores, axis=1, keepdims=True)
            weights = jnp.exp2((scores - height) * EXP_SCALE).astype(BF16)
            pieces.append((dot(weights, values), jnp.broadcast_to(height, (block, LANES))))
        own_val[pair], own_lse[pair] = finish(pieces)
        return unused

    lax.fori_loop(0, pairs, own_attention, 0)

    own_copies[0].wait()
    own_copies[1].wait()

    def kv_wait(slot, source):
        pltpu.make_async_remote_copy(
            src_ref=place(slot, source),
            dst_ref=place(slot, source),
            send_sem=kv_send.at[slot, source],
            recv_sem=kv_recv.at[slot, source],
            device_id={"patch": source},
            device_id_type=MESH,
        ).wait_recv()

    def receive_kv(step, unused):
        source = lax.rem(me + step, size)
        kv_wait(0, source)

        @pl.when(my_last != my_first)
        def _():
            kv_wait(1, source)

        return unused

    lax.fori_loop(1, size, receive_kv, 0)

    def run_task(index, unused):
        task = me * pairs + index
        pair = lax.div(task, size)
        owner = lax.rem(task, size)
        slot = pair - my_first
        pltpu.make_async_copy(q_in.at[index], q_in.at[index], q_recv.at[index]).wait()
        queries = heads_of(q_in[index])

        def partial(step):
            at = pl.ds(pl.multiple_of(lax.rem(owner + step, size) * block, block), block)
            return kvs[slot, 0, at, :], jnp.concatenate([kvs[slot, 1, at, :], ones], axis=1)

        keys, values = partial(1)
        for head in range(2):
            scores = scores_of(queries[head], keys)
            height = jnp.max(scores, axis=1, keepdims=True)
            weights = jnp.exp2((scores - height) * EXP_SCALE).astype(BF16)
            acc[head] = dot(weights, values)
            top[head] = jnp.broadcast_to(height, (block, LANES))

        def more(step, unused):
            keys, values = partial(step)
            for head in range(2):
                scores = scores_of(queries[head], keys)
                before = top[head]
                height = jnp.maximum(before, jnp.max(scores, axis=1, keepdims=True))
                factor = jnp.exp2((before - height) * EXP_SCALE)
                weights = jnp.exp2((scores - height[:, :1]) * EXP_SCALE).astype(BF16)
                summed = dot(weights, values)
                acc[head, :, :LANES] = acc[head, :, :LANES] * factor + summed[:, :LANES]
                acc[head, :, LANES:] = acc[head, :, LANES:] * factor + summed[:, LANES:]
                top[head] = height
            return unused

        lax.fori_loop(2, size, more, 0)
        value, lse = finish([(acc[0], top[0]), (acc[1], top[1])])
        res[index] = value.astype(BF16)
        turned = jnp.transpose(lse)
        res_lse[index, 0:8] = turned[0:8]
        res_lse[index, 8:16] = turned[HEAD_DIM : HEAD_DIM + 8]

        @pl.when(owner != me)
        def _():
            for copy in result_copies(index, pair, owner):
                copy.start()

        @pl.when(owner == me)
        def _():
            pltpu.make_async_copy(res.at[index], res_in.at[pair], res_recv.at[pair]).start()
            pltpu.make_async_copy(res_lse.at[index], lse_in.at[pair], lse_recv.at[pair]).start()

        return unused

    def result_copies(index, pair, owner):
        return [
            pltpu.make_async_remote_copy(
                src_ref=source.at[index],
                dst_ref=into.at[pair],
                send_sem=sent.at[index],
                recv_sem=received.at[pair],
                device_id={"patch": owner},
                device_id_type=MESH,
            )
            for source, into, sent, received in (
                (res, res_in, res_send, res_recv),
                (res_lse, lse_in, lse_send, lse_recv),
            )
        ]

    lax.fori_loop(0, pairs, run_task, 0)

    output = mixed[...]
    for pair in range(pairs):
        pltpu.make_async_copy(res_in.at[pair], res_in.at[pair], res_recv.at[pair]).wait()
        pltpu.make_async_copy(lse_in.at[pair], lse_in.at[pair], lse_recv.at[pair]).wait()
    merged = []
    for pair in range(pairs):
        rows = lax.broadcasted_iota(jnp.int32, (LANES, block), 0) < HEAD_DIM
        lse = jnp.transpose(jnp.where(rows, lse_in[pair, 0:1], lse_in[pair, 8:9]))
        mine = own_lse[pair]
        best = jnp.maximum(lse, mine)
        there = jnp.exp(lse - best)
        here = jnp.exp(mine - best)
        value = (there * res_in[pair].astype(F32) + here * own_val[pair]) / (there + here)
        merged.append(value.astype(BF16))
    out_ref[...] = (output + dot(jnp.concatenate(merged, axis=1), projw[3])).astype(BF16)

    def sent_kv(step, unused):
        target = lax.rem(me + step, size)
        kv_copy(0, first_pair(target), target, me).wait_send()

        @pl.when(last_pair(target) != first_pair(target))
        def _():
            kv_copy(1, last_pair(target), target, me).wait_send()

        return unused

    lax.fori_loop(1, size, sent_kv, 0)
    for pair in range(pairs):
        target, slot = task_of(pair)

        @pl.when(target != me)
        def _():
            q_remote(pair, target, slot).wait_send()

        task = me * pairs + pair
        owner = lax.rem(task, size)

        @pl.when(owner != me)
        def _():
            for copy in result_copies(pair, lax.div(task, size), owner):
                copy.wait_send()


def on_device(
    features,
    stale_kv,
    timestep,
    time_w,
    gain_one,
    conv_w,
    shortcut_w,
    gain_two,
    query_w,
    key_w,
    value_w,
    out_w,
):
    rows, cols, width_in = features.shape
    width = shortcut_w.shape[1]
    block = rows * cols
    size = lax.axis_size("patch")
    pairs = width // LANES
    half = FREQ // 2
    freqs = jnp.exp(-math.log(10000.0) * jnp.arange(half, dtype=F32) / half)
    angles = timestep.astype(F32)[0] * freqs
    embed = jnp.concatenate([jnp.cos(angles), jnp.sin(angles)]).astype(BF16)
    embed = jnp.broadcast_to(embed[None, :], (16, FREQ))
    anywhere = pl.BlockSpec(memory_space=pl.ANY)
    vmem = pl.BlockSpec(memory_space=pltpu.VMEM)
    dma = pltpu.SemaphoreType.DMA
    flops = 2 * block * width * (10 * width_in + 4 * width + 4 * size * block)
    output = pl.pallas_call(
        functools.partial(fused_kernel, size),
        out_shape=jax.ShapeDtypeStruct((block, width), BF16),
        in_specs=[anywhere, anywhere, vmem, vmem, vmem, anywhere, anywhere, vmem]
        + [anywhere] * 4,
        out_specs=vmem,
        scratch_shapes=[
            pltpu.VMEM((block, width_in), BF16),
            pltpu.VMEM((3, 3, width_in, width), BF16),
            pltpu.VMEM((width_in, width), BF16),
            pltpu.VMEM((4, width, width), BF16),
            pltpu.VMEM((block + 2 * cols, width_in), BF16),
            pltpu.VMEM((3, block, width), F32),
            pltpu.VMEM((block, width), F32),
            pltpu.VMEM((2, 2, size * block, LANES), BF16),
            pltpu.VMEM((8, width_in), F32),
            pltpu.VMEM((size, 8, width_in), F32),
            pltpu.VMEM((8, width), F32),
            pltpu.VMEM((size, 8, width), F32),
            pltpu.VMEM((3, pairs, block, LANES), BF16),
            pltpu.VMEM((pairs, block, LANES), BF16),
            pltpu.VMEM((pairs, block, LANES), F32),
            pltpu.VMEM((pairs, block, LANES), F32),
            pltpu.VMEM((2, block, 2 * LANES), F32),
            pltpu.VMEM((2, block, LANES), F32),
            pltpu.VMEM((pairs, block, LANES), BF16),
            pltpu.VMEM((pairs, 16, block), F32),
            pltpu.VMEM((pairs, block, LANES), BF16),
            pltpu.VMEM((pairs, 16, block), F32),
            dma((6,)),
            dma((3, 3)),
            dma((2, size)),
            dma((2, size)),
            dma((2,)),
            dma((2, size)),
            dma((2, size)),
            dma((2,)),
            dma((2,)),
            dma((pairs,)),
            dma((pairs,)),
            dma((pairs,)),
            dma((pairs,)),
            dma((pairs,)),
            dma((pairs,)),
        ],
        compiler_params=pltpu.CompilerParams(
            collective_id=0, has_side_effects=True, vmem_limit_bytes=58 * 1024 * 1024
        ),
        cost_estimate=pl.CostEstimate(
            flops=flops, bytes_accessed=24_000_000, transcendentals=block * size * block * 10
        ),
    )(
        stale_kv,
        features.reshape(block, width_in),
        embed,
        time_w,
        gain_one[None, :],
        conv_w,
        shortcut_w,
        gain_two[None, :],
        query_w,
        key_w,
        value_w,
        out_w,
    )
    return output.reshape(rows, cols, width)


def solution(mesh):
    return jax.shard_map(
        on_device,
        mesh=mesh,
        in_specs=(
            P("patch", "batch", None),
            P("batch", "patch", None),
            P("batch"),
            P(),
            P(),
            P(),
            P(),
            P(),
            P(),
            P(),
            P(),
            P(),
        ),
        out_specs=P("patch", "batch", None),
        check_vma=False,
    )
```

time: 277 us -> 135 us (0.49)
  Pallas kernels: 0 us -> 129 us
  matrix products: 86.6 us -> 0 us
  blocking collectives: 58.1 us -> 0 us
  local copies, waits for them, and re-layouts: 59.7 us -> 5.03 us
  waiting for transfers between devices: 34 us -> 0 us
  other arithmetic: 15.1 us -> 0.13 us
  between operations: 14.4 us -> 0.67 us
  loops' own time: 5.51 us -> 0 us
    pallas_call x0 -> x1, Pallas kernels: none -> 129 us  [on_device(): pl.pallas_call(functools.partial(fused_kernel, size), out_shape=jax.Shape...]
    dot_general x33 -> x0, matrix products: 86.6 us -> none  [the longest x9 44.4 us: block_partial(): jnp.einsum('hqk,khd->hqd', expo.astype(jnp.bfloat16), values, preferred_e...]
    psum x2 -> x0, blocking collectives: 58.1 us -> none  [normalize(): lax.psum((jnp.sum(grouped, axis=(0, 2)), jnp.sum(grouped * grouped, axis=...]
    all_gather x1 -> x0, waiting for transfers between devices: 33.2 us -> none  [on_device(): piece = lax.all_gather(stale_kv, 'patch', axis=1, tiled=True)]
    while x16 -> x0, local copies, waits for them, and re-layouts: 20.6 us -> none
    slice x5 -> x0, local copies, waits for them, and re-layouts: 19.7 us -> none  [the longest x2 11.9 us: on_device(): value_rows = piece[1].reshape(pieces, block, heads, HEAD_DIM)]
    reduce_sum x14 -> x0, other arithmetic: 10.8 us -> none  [the longest x9 8.81 us: block_partial(): total = jnp.sum(expo, axis=2)]
    unnamed x20 -> x1, local copies, waits for them, and re-layouts: 11.8 us -> 1.85 us
  transfers between devices with their start and end apart: 3 -> 0, of which waited for: 2 -> 0; matrix products, arithmetic and copies ran while one was open for 13% -> 0% of each run, Pallas kernels for 0% -> 0%
where the time goes in v1:
time: 135 us
  Pallas kernels  129 us (96%)
  local copies, waits for them, and re-layouts  5.03 us (4%)
    pallas_call x1, Pallas kernels, on_device(): pl.pallas_call(functools.partial(fused_kernel, size), out_shape=jax.Shape...  129 us

profile of v1, /device:TPU:0, one launch (start us, length us, event | category | flops | bytes accessed | tf_op | source)
XLA Modules:
  0.0 134.8 jit_solution(9583964433477667028)
XLA Ops:
  0.7 0.1 sine_convert_fusion
  0.7 0.1 pad_maximum_fusion
  0.8 1.3 broadcast_in_dim.14.gain_two_ref
  2.1 1.3 broadcast_in_dim.13.gain_one_ref
  3.4 0.6 broadcast_in_dim.12.embed_ref
  4.0 129.0 %shard_map.118 = bf16[384,640]{1,0:T(8,128)(2,1)} custom-call(bf16[2,384,640]{2,1,0:T(8,128)(2,1)} %kv_ref.1, bf16[384,1280]{1,0:T(8,128)(2,1)} %bitcast.4, bf16[16,320]{1,0:T(8,128)(2,1)} %broadcast_in_dim.12.embed_ref, bf16[320,640]{1,0:T(8,128)(2,1)} %time_ref.1, f32[1,1280]{1,0:T(1,128)} %broadcast_in_dim.13.gain_one_ref, ...), custom_call_target="tpu_custom_call" | custom-call | flops 13589544960 | bytes 24000000 | tf_op jit(solution)/shard_map/pallas_call | solution.py:583
  133.0 1.9 %copy.15 = bf16[3,128,640]{2,1,0:T(8,128)(2,1)} copy(bf16[3,128,640]{2,1,0:T(8,128)(2,1)} %bitcast.3) | data formatting | bytes 983040

commit v2 on v1

v2 whole, which is shorter than its diff:
```python
import functools
import math

import jax
import jax.numpy as jnp
from jax import lax
from jax.experimental import pallas as pl
from jax.experimental.pallas import tpu as pltpu
from jax.sharding import PartitionSpec as P

HEAD_DIM = 64
GROUPS = 32
FREQ = 320
LANES = 128
F32 = jnp.float32
BF16 = jnp.bfloat16
EXP_SCALE = 0.125 * math.log2(math.e)
LN2 = math.log(2.0)
MESH = pl.DeviceIdType.MESH


def dot(a, b):
    return jnp.dot(a, b, preferred_element_type=F32)


def split_dot(a, b):
    high = a.astype(BF16)
    rest = a - high.astype(F32)
    mid = rest.astype(BF16)
    low = rest - mid.astype(F32)
    stacked = jnp.concatenate([high.astype(F32), mid.astype(F32), low, jnp.zeros_like(a)], axis=0)
    out = dot(stacked.astype(BF16), b)
    return out[0:8] + out[8:16] + out[16:24]


def swap(x):
    return pltpu.roll(x.astype(F32), HEAD_DIM, 1)


def fold(x, side):
    rows = x.shape[0] // 2
    upper, lower = x[:rows].astype(F32), x[rows:].astype(F32)
    mask = half_mask(rows)
    if side == 0:
        return jnp.where(mask, upper, swap(lower)).astype(BF16)
    return jnp.where(mask, swap(upper), lower).astype(BF16)


def members(shape, chan_dim, size):
    chan = lax.broadcasted_iota(jnp.int32, shape, chan_dim)
    group = lax.broadcasted_iota(jnp.int32, shape, 1 - chan_dim) * size
    return jnp.where((chan >= group) & (chan < group + size), 1.0, 0.0).astype(BF16)


def two_rows(first, second):
    row = lax.broadcasted_iota(jnp.int32, (8, first.shape[1]), 0)
    return jnp.where(row == 0, first, jnp.where(row == 1, second, 0.0))


def group_sums(total):
    width = total.shape[1]
    return split_dot(total, members((width, LANES), 0, width // GROUPS))


def group_stats(grouped, count, width, eps):
    center = grouped[0:1] / count
    spread = jnp.maximum(grouped[1:2] / count - center * center, 0.0)
    size = width // GROUPS
    wide = split_dot(two_rows(center, lax.rsqrt(spread + eps)), members((LANES, width), 1, size))
    return wide[0:1], wide[1:2]


def half_mask(rows):
    return lax.broadcasted_iota(jnp.int32, (rows, LANES), 1) < HEAD_DIM


def scores_of(query, keys):
    return lax.dot_general(query, keys, (((1,), (1,)), ((), ())), preferred_element_type=F32)


def fused_kernel(
    size,
    kv_ref,
    feat_ref,
    embed_ref,
    time_ref,
    gain_one_ref,
    conv_ref,
    short_ref,
    gain_two_ref,
    qw_ref,
    kw_ref,
    vw_ref,
    ow_ref,
    out_ref,
    feat,
    convw,
    shortw,
    projw,
    act,
    parts,
    mixed,
    kvs,
    stale,
    packed,
    stat_out1,
    stat_in1,
    stat_out2,
    stat_in2,
    fresh,
    q_out,
    q_in,
    own_val,
    own_lse,
    acc,
    top,
    res,
    res_lse,
    res_in,
    lse_in,
    load_sem,
    conv_sem,
    kv_send,
    kv_recv,
    stat_send,
    stat_recv,
    halo_send,
    halo_recv,
    q_send,
    q_recv,
    res_send,
    res_recv,
    lse_send,
    lse_recv,
):
    me = lax.axis_index("patch")
    block, width = out_ref.shape
    width_in = feat.shape[1]
    pairs = width // LANES
    heads = width // HEAD_DIM
    slots = kvs.shape[0]
    cols = (act.shape[0] - block) // 2
    inside = pl.ds(cols, block)

    loads = [
        pltpu.make_async_copy(feat_ref, feat.at[pl.ds(cols, block), :], load_sem.at[0]),
        pltpu.make_async_copy(short_ref, shortw, load_sem.at[1]),
        pltpu.make_async_copy(qw_ref, projw.at[0], load_sem.at[2]),
        pltpu.make_async_copy(kw_ref, projw.at[1], load_sem.at[3]),
        pltpu.make_async_copy(vw_ref, projw.at[2], load_sem.at[4]),
        pltpu.make_async_copy(ow_ref, projw.at[3], load_sem.at[5]),
    ]
    conv_loads = [
        [
            pltpu.make_async_copy(conv_ref.at[dy, dx], convw.at[dy, dx], conv_sem.at[dy, dx])
            for dx in range(3)
        ]
        for dy in range(3)
    ]
    stale_load = pltpu.make_async_copy(kv_ref, stale, load_sem.at[6])
    stale_load.start()
    loads[0].start()
    loads[1].start()
    for dy in (1, 0, 2):
        for dx in range(3):
            conv_loads[dy][dx].start()
    for load in loads[2:]:
        load.start()

    barrier = pltpu.get_barrier_semaphore()

    def greet(step, unused):
        pl.semaphore_signal(
            barrier, inc=1, device_id={"patch": lax.rem(me + step, size)}, device_id_type=MESH
        )
        return unused

    lax.fori_loop(1, size, greet, 0)

    def first_head(device):
        return lax.div(device * heads, size)

    def last_head(device):
        return lax.div(device * heads + heads - 1, size)

    def place(slot, owner):
        return kvs.at[slot, pl.ds(pl.multiple_of(owner * block, block), block), :]

    def kv_copy(slot, target):
        return pltpu.make_async_remote_copy(
            src_ref=packed.at[first_head(target) + slot],
            dst_ref=place(slot, me),
            send_sem=kv_send.at[slot, target],
            recv_sem=kv_recv.at[slot, me],
            device_id={"patch": target},
            device_id_type=MESH,
        )

    my_first = first_head(me)
    my_last = last_head(me)

    def pack_kv(step, unused):
        lanes = pl.ds(pl.multiple_of(step * LANES, LANES), LANES)
        keys = stale[0, :, lanes].astype(F32)
        values = stale[1, :, lanes].astype(F32)
        mask = half_mask(block)
        packed[2 * step] = jnp.where(mask, keys, swap(values)).astype(BF16)
        packed[2 * step + 1] = jnp.where(mask, swap(keys), values).astype(BF16)
        return unused

    stale_load.wait()
    lax.fori_loop(0, pairs, pack_kv, 0)
    for slot in range(slots):

        @pl.when(my_first + slot <= my_last)
        def _():
            kvs[slot, pl.ds(pl.multiple_of(me * block, block), block), :] = packed[my_first + slot]


    loads[0].wait()

    @pl.when(me == 0)
    def _():
        feat[0:cols, :] = jnp.zeros((cols, width_in), BF16)

    @pl.when(me == size - 1)
    def _():
        feat[block + cols : block + 2 * cols, :] = jnp.zeros((cols, width_in), BF16)

    def sum_rows(step, carry):
        first, second = carry
        x = feat[pl.ds(pl.multiple_of(cols + step * 16, 16), 16), :].astype(F32)
        low, high = x[:8], x[8:]
        return first + (low + high), second + (low * low + high * high)

    zero = jnp.zeros((8, width_in), F32)
    first, second = lax.fori_loop(0, block // 16, sum_rows, (zero, zero))
    sums = two_rows(
        jnp.sum(first, axis=0, keepdims=True), jnp.sum(second, axis=0, keepdims=True)
    )
    stat_out1[...] = group_sums(sums)
    pl.semaphore_wait(barrier, size - 1)

    def stat_copy(which, out, into, target, index):
        return pltpu.make_async_remote_copy(
            src_ref=out,
            dst_ref=into.at[me],
            send_sem=stat_send.at[which, target],
            recv_sem=stat_recv.at[which, index],
            device_id={"patch": target},
            device_id_type=MESH,
        )

    def stats_start(which, out, into):
        def send(step, unused):
            target = lax.rem(me + step, size)
            stat_copy(which, out, into, target, me).start()
            return unused

        lax.fori_loop(1, size, send, 0)

    def stats_finish(which, out, into):
        def receive(step, total):
            source = lax.rem(me + step, size)
            pltpu.make_async_remote_copy(
                src_ref=out,
                dst_ref=into.at[source],
                send_sem=stat_send.at[which, source],
                recv_sem=stat_recv.at[which, source],
                device_id={"patch": source},
                device_id_type=MESH,
            ).wait()
            return total + into[source]

        return lax.fori_loop(1, size, receive, out[...])

    stats_start(0, stat_out1, stat_in1)

    top_row = feat.at[pl.ds(cols, cols), :]
    bottom_row = feat.at[pl.ds(block, cols), :]
    above = feat.at[pl.ds(0, cols), :]
    below = feat.at[pl.ds(block + cols, cols), :]
    up = pltpu.make_async_remote_copy(
        src_ref=top_row,
        dst_ref=below,
        send_sem=halo_send.at[0],
        recv_sem=halo_recv.at[0],
        device_id={"patch": lax.rem(me + size - 1, size)},
        device_id_type=MESH,
    )
    down = pltpu.make_async_remote_copy(
        src_ref=bottom_row,
        dst_ref=above,
        send_sem=halo_send.at[1],
        recv_sem=halo_recv.at[1],
        device_id={"patch": lax.rem(me + 1, size)},
        device_id_type=MESH,
    )

    @pl.when(me > 0)
    def _():
        up.start()

    @pl.when(me < size - 1)
    def _():
        down.start()

    def send_kv(step, unused):
        target = lax.rem(me + step, size)
        kv_copy(0, target).start()
        for slot in range(1, slots):

            @pl.when(first_head(target) + slot <= last_head(target))
            def _():
                kv_copy(slot, target).start()

        return unused

    lax.fori_loop(1, size, send_kv, 0)

    loads[1].wait()
    mixed[...] = dot(feat[inside, :], shortw[...]) + dot(embed_ref[...], time_ref[...])[0:1]

    total = stats_finish(0, stat_out1, stat_in1)
    count = float(size * block * (width_in // GROUPS))
    center, inverse = group_stats(total, count, width_in, 1e-05)
    scale = inverse * gain_one_ref[...].reshape(1, width_in)

    @pl.when(me > 0)
    def _():
        up.wait_send()
        down.wait_recv()

    @pl.when(me < size - 1)
    def _():
        down.wait_send()
        up.wait_recv()

    def activate(step, unused):
        x = feat[pl.ds(pl.multiple_of(step * 16, 16), 16), :].astype(F32)
        y = (x - center) * scale
        half = 0.5 * y
        z = half + half * jnp.tanh(half)
        act[pl.ds(pl.multiple_of(step * 16, 16), 16), :] = z.astype(BF16)
        return unused

    lax.fori_loop(0, act.shape[0] // 16, activate, 0)

    @pl.when(me == 0)
    def _():
        act[0:cols, :] = jnp.zeros((cols, width_in), BF16)

    @pl.when(me == size - 1)
    def _():
        act[block + cols : block + 2 * cols, :] = jnp.zeros((cols, width_in), BF16)

    for dx in range(3):
        conv_loads[1][dx].wait()

    def middle(dx, unused):
        parts[dx] = dot(act[pl.ds(cols, block), :], convw[1, dx])
        return unused

    lax.fori_loop(0, 3, middle, 0)

    for dy in (0, 2):
        for dx in range(3):
            conv_loads[dy][dx].wait()

    def outer(dx, unused):
        parts[dx] = (
            parts[dx]
            + dot(act[pl.ds(0, block), :], convw[0, dx])
            + dot(act[pl.ds(2 * cols, block), :], convw[2, dx])
        )
        return unused

    lax.fori_loop(0, 3, outer, 0)

    col = lax.rem(lax.broadcasted_iota(jnp.int32, (block, LANES), 0), cols)
    sums = []
    for pair in range(pairs):
        lanes = pl.ds(pair * LANES, LANES)
        left = jnp.where(col == 0, 0.0, pltpu.roll(parts[0, :, lanes], 1, 0))
        right = jnp.where(col == cols - 1, 0.0, pltpu.roll(parts[2, :, lanes], block - 1, 0))
        value = mixed[:, lanes] + (left + parts[1, :, lanes] + right)
        mixed[:, lanes] = value
        sums.append(
            two_rows(
                jnp.sum(value, axis=0, keepdims=True),
                jnp.sum(value * value, axis=0, keepdims=True),
            )
        )
    stat_out2[...] = group_sums(jnp.concatenate(sums, axis=1))
    stats_start(1, stat_out2, stat_in2)
    for load in loads[2:]:
        load.wait()
    total = stats_finish(1, stat_out2, stat_in2)
    count = float(size * block * (width // GROUPS))
    center, inverse = group_stats(total, count, width, 1e-06)
    normed = ((mixed[...] - center) * (inverse * gain_two_ref[...].reshape(1, width))).astype(BF16)

    def task_of(head):
        task = head * size + me
        return lax.div(task, heads), lax.rem(task, heads)

    def q_remote(head, target, slot):
        return pltpu.make_async_remote_copy(
            src_ref=q_out.at[head],
            dst_ref=q_in.at[slot],
            send_sem=q_send.at[head],
            recv_sem=q_recv.at[slot],
            device_id={"patch": target},
            device_id_type=MESH,
        )

    queries = dot(normed, projw[0]).astype(BF16)
    for pair in range(pairs):
        both = queries[:, pair * LANES : (pair + 1) * LANES]
        fresh[0, pair] = both
        q_out[2 * pair] = fold(both, 0)
        q_out[2 * pair + 1] = fold(both, 1)

    def send_queries(head, unused):
        target, slot = task_of(head)

        @pl.when(target != me)
        def _():
            q_remote(head, target, slot).start()

        @pl.when(target == me)
        def _():
            pltpu.make_async_copy(q_out.at[head], q_in.at[slot], q_recv.at[slot]).start()

        return unused

    lax.fori_loop(0, heads, send_queries, 0)

    for kind in (1, 2):
        value = dot(normed, projw[kind]).astype(BF16)
        for pair in range(pairs):
            fresh[kind, pair] = value[:, pair * LANES : (pair + 1) * LANES]

    left_half = half_mask(block)
    ones = jnp.ones((block, LANES), BF16)

    def heads_of(query):
        none = jnp.zeros_like(query)
        return jnp.where(left_half, query, none), jnp.where(left_half, none, query)

    def finish(pieces):
        values, lses = [], []
        for summed, height in pieces:
            weight = summed[:, LANES:]
            values.append(summed[:, :LANES] / weight)
            lses.append(height * 0.125 + jnp.log(weight))
        return jnp.where(left_half, *values), jnp.where(left_half, *lses)

    def own_attention(pair, unused):
        keys = fresh[1, pair]
        values = jnp.concatenate([fresh[2, pair], ones], axis=1)
        pieces = []
        for query in heads_of(fresh[0, pair]):
            scores = scores_of(query, keys)
            height = jnp.max(scores, axis=1, keepdims=True)
            weights = jnp.exp2((scores - height) * EXP_SCALE).astype(BF16)
            pieces.append((dot(weights, values), jnp.broadcast_to(height, (block, LANES))))
        own_val[pair], own_lse[pair] = finish(pieces)
        return unused

    lax.fori_loop(0, pairs, own_attention, 0)

    def kv_wait(slot, source):
        pltpu.make_async_remote_copy(
            src_ref=place(slot, source),
            dst_ref=place(slot, source),
            send_sem=kv_send.at[slot, source],
            recv_sem=kv_recv.at[slot, source],
            device_id={"patch": source},
            device_id_type=MESH,
        ).wait_recv()

    def receive_kv(step, unused):
        source = lax.rem(me + step, size)
        kv_wait(0, source)
        for slot in range(1, slots):

            @pl.when(my_first + slot <= my_last)
            def _():
                kv_wait(slot, source)

        return unused

    lax.fori_loop(1, size, receive_kv, 0)

    def place_of(index):
        task = me * heads + index
        return lax.div(task, size), lax.rem(task, size)

    def unfold(x):
        mask = half_mask(block // 2)
        upper = jnp.where(mask, x.astype(F32), 0.0)
        lower = jnp.where(mask, swap(x), 0.0)
        return jnp.concatenate([upper, lower], axis=0).astype(BF16)

    def run_tasks(couple, unused):
        tasks = []
        for which in range(2):
            index = 2 * couple + which
            head, owner = place_of(index)
            pltpu.make_async_copy(q_in.at[index], q_in.at[index], q_recv.at[index]).wait()
            tasks.append((head - my_first, owner, unfold(q_in[index])))

        def partial(slot, owner, step):
            rows = pl.ds(pl.multiple_of(lax.rem(owner + step, size) * block, block), block)
            both = kvs[slot, rows, :]
            return both, jnp.where(left_half, ones, both)

        for which, (slot, owner, query) in enumerate(tasks):
            keys, values = partial(slot, owner, 1)
            scores = scores_of(query, keys)
            height = jnp.max(scores, axis=1, keepdims=True)
            weights = jnp.exp2((scores - height) * EXP_SCALE).astype(BF16)
            acc[which] = dot(weights, values)
            top[which] = jnp.broadcast_to(height, (block, LANES))

        def more(step, unused):
            for which, (slot, owner, query) in enumerate(tasks):
                keys, values = partial(slot, owner, step)
                scores = scores_of(query, keys)
                before = top[which]
                height = jnp.maximum(before, jnp.max(scores, axis=1, keepdims=True))
                factor = jnp.exp2((before - height) * EXP_SCALE)
                weights = jnp.exp2((scores - height[:, :1]) * EXP_SCALE).astype(BF16)
                acc[which] = acc[which] * factor + dot(weights, values)
                top[which] = height
            return unused

        lax.fori_loop(2, size, more, 0)
        lses = []
        for which in range(2):
            index = 2 * couple + which
            summed = acc[which]
            total = swap(summed)
            res[index] = fold(summed / total, 1)
            lses.append(top[which] * 0.125 + jnp.log(total))
        turned = jnp.transpose(jnp.where(left_half, swap(lses[0]), lses[1]))
        res_lse[2 * couple] = turned[0:8]
        res_lse[2 * couple + 1] = turned[HEAD_DIM : HEAD_DIM + 8]
        for which in range(2):
            index = 2 * couple + which
            head, owner = place_of(index)

            @pl.when(owner != me)
            def _():
                for copy in result_copies(index, head, owner):
                    copy.start()

            @pl.when(owner == me)
            def _():
                pltpu.make_async_copy(res.at[index], res_in.at[head], res_recv.at[head]).start()
                pltpu.make_async_copy(
                    res_lse.at[index], lse_in.at[head], lse_recv.at[head]
                ).start()

        return unused

    def result_copies(index, head, owner):
        return [
            pltpu.make_async_remote_copy(
                src_ref=source.at[index],
                dst_ref=into.at[head],
                send_sem=sent.at[index],
                recv_sem=received.at[head],
                device_id={"patch": owner},
                device_id_type=MESH,
            )
            for source, into, sent, received in (
                (res, res_in, res_send, res_recv),
                (res_lse, lse_in, lse_send, lse_recv),
            )
        ]

    lax.fori_loop(0, pairs, run_tasks, 0)

    output = mixed[...]
    for pair in range(heads):
        pltpu.make_async_copy(res_in.at[pair], res_in.at[pair], res_recv.at[pair]).wait()
        pltpu.make_async_copy(lse_in.at[pair], lse_in.at[pair], lse_recv.at[pair]).wait()
    merged = []
    for pair in range(pairs):
        rows = lax.broadcasted_iota(jnp.int32, (LANES, block), 0) < HEAD_DIM
        lse = jnp.transpose(jnp.where(rows, lse_in[2 * pair, 0:1], lse_in[2 * pair + 1, 0:1]))
        mine = own_lse[pair]
        best = jnp.maximum(lse, mine)
        there = jnp.exp(lse - best)
        here = jnp.exp(mine - best)
        first, second = res_in[2 * pair].astype(F32), res_in[2 * pair + 1].astype(F32)
        mask = half_mask(block // 2)
        upper = jnp.where(mask, first, swap(second))
        lower = jnp.where(mask, swap(first), second)
        value = (there * jnp.concatenate([upper, lower], axis=0) + here * own_val[pair]) / (there + here)
        merged.append(value.astype(BF16))
    out_ref[...] = (output + dot(jnp.concatenate(merged, axis=1), projw[3])).astype(BF16)

    def sent_kv(step, unused):
        target = lax.rem(me + step, size)
        kv_copy(0, target).wait_send()
        for slot in range(1, slots):

            @pl.when(first_head(target) + slot <= last_head(target))
            def _():
                kv_copy(slot, target).wait_send()

        return unused

    lax.fori_loop(1, size, sent_kv, 0)

    def sent_rest(index, unused):
        target, slot = task_of(index)

        @pl.when(target != me)
        def _():
            q_remote(index, target, slot).wait_send()

        head, owner = place_of(index)

        @pl.when(owner != me)
        def _():
            for copy in result_copies(index, head, owner):
                copy.wait_send()

        return unused

    lax.fori_loop(0, heads, sent_rest, 0)


def slots_for(heads, size):
    return max(
        (device * heads + heads - 1) // size - device * heads // size + 1
        for device in range(size)
    )


def on_device(
    features,
    stale_kv,
    timestep,
    time_w,
    gain_one,
    conv_w,
    shortcut_w,
    gain_two,
    query_w,
    key_w,
    value_w,
    out_w,
):
    rows, cols, width_in = features.shape
    width = shortcut_w.shape[1]
    block = rows * cols
    size = lax.axis_size("patch")
    pairs = width // LANES
    heads = width // HEAD_DIM
    half = FREQ // 2
    freqs = jnp.exp(-math.log(10000.0) * jnp.arange(half, dtype=F32) / half)
    angles = timestep.astype(F32)[0] * freqs
    embed = jnp.concatenate([jnp.cos(angles), jnp.sin(angles)]).astype(BF16)
    embed = jnp.broadcast_to(embed[None, :], (16, FREQ))
    anywhere = pl.BlockSpec(memory_space=pl.ANY)
    vmem = pl.BlockSpec(memory_space=pltpu.VMEM)
    dma = pltpu.SemaphoreType.DMA
    flops = 2 * block * width * (10 * width_in + 4 * width + 4 * size * block)
    output = pl.pallas_call(
        functools.partial(fused_kernel, size),
        out_shape=jax.ShapeDtypeStruct((block, width), BF16),
        in_specs=[anywhere, anywhere, vmem, vmem, vmem, anywhere, anywhere, vmem]
        + [anywhere] * 4,
        out_specs=vmem,
        scratch_shapes=[
            pltpu.VMEM((block + 2 * cols, width_in), BF16),
            pltpu.VMEM((3, 3, width_in, width), BF16),
            pltpu.VMEM((width_in, width), BF16),
            pltpu.VMEM((4, width, width), BF16),
            pltpu.VMEM((block + 2 * cols, width_in), BF16),
            pltpu.VMEM((3, block, width), F32),
            pltpu.VMEM((block, width), F32),
            pltpu.VMEM((slots_for(heads, size), size * block, LANES), BF16),
            pltpu.VMEM((2, block, width), BF16),
            pltpu.VMEM((heads, block, LANES), BF16),
            pltpu.VMEM((8, LANES), F32),
            pltpu.VMEM((size, 8, LANES), F32),
            pltpu.VMEM((8, LANES), F32),
            pltpu.VMEM((size, 8, LANES), F32),
            pltpu.VMEM((3, pairs, block, LANES), BF16),
            pltpu.VMEM((heads, block // 2, LANES), BF16),
            pltpu.VMEM((heads, block // 2, LANES), BF16),
            pltpu.VMEM((pairs, block, LANES), F32),
            pltpu.VMEM((pairs, block, LANES), F32),
            pltpu.VMEM((2, block, LANES), F32),
            pltpu.VMEM((2, block, LANES), F32),
            pltpu.VMEM((heads, block // 2, LANES), BF16),
            pltpu.VMEM((heads, 8, block), F32),
            pltpu.VMEM((heads, block // 2, LANES), BF16),
            pltpu.VMEM((heads, 8, block), F32),
            dma((7,)),
            dma((3, 3)),
            dma((slots_for(heads, size), size)),
            dma((slots_for(heads, size), size)),
            dma((2, size)),
            dma((2, size)),
            dma((2,)),
            dma((2,)),
            dma((heads,)),
            dma((heads,)),
            dma((heads,)),
            dma((heads,)),
            dma((heads,)),
            dma((heads,)),
        ],
        compiler_params=pltpu.CompilerParams(
            collective_id=0, has_side_effects=True, vmem_limit_bytes=58 * 1024 * 1024
        ),
        cost_estimate=pl.CostEstimate(
            flops=flops, bytes_accessed=24_000_000, transcendentals=block * size * block * 10
        ),
    )(
        stale_kv,
        features.reshape(block, width_in),
        embed,
        time_w,
        gain_one,
        conv_w,
        shortcut_w,
        gain_two,
        query_w,
        key_w,
        value_w,
        out_w,
    )
    return output.reshape(rows, cols, width)


def solution(mesh):
    return jax.shard_map(
        on_device,
        mesh=mesh,
        in_specs=(
            P("patch", "batch", None),
            P("batch", "patch", None),
            P("batch"),
            P(),
            P(),
            P(),
            P(),
            P(),
            P(),
            P(),
            P(),
            P(),
        ),
        out_specs=P("patch", "batch", None),
        check_vma=False,
    )
```

time: 135 us -> 118 us (0.87)
  Pallas kernels: 129 us -> 114 us
  local copies, waits for them, and re-layouts: 5.03 us -> 2.46 us
    pallas_call x1, Pallas kernels: 129 us -> 114 us  [on_device(): pl.pallas_call(functools.partial(fused_kernel, size), out_shape=jax.Shape...]
    broadcast_in_dim x2 -> x0, local copies, waits for them, and re-layouts: 2.57 us -> none  [the longest x1 1.29 us: on_device(): gain_two[None, :]]
where the time goes in v2:
time: 118 us; the launch traced here: 117 us
  Pallas kernels  114 us (97%)
  local copies, waits for them, and re-layouts  2.46 us (2%)
    pallas_call x1, Pallas kernels, on_device(): pl.pallas_call(functools.partial(fused_kernel, size), out_shape=jax.Shape...  114 us

profile of v2, /device:TPU:0, one launch (start us, length us, event | category | flops | bytes accessed | tf_op | source)
XLA Modules:
  0.0 117.3 jit_solution(13292783053756564970)
XLA Ops:
  0.7 0.1 sine_convert_fusion
  0.7 0.1 pad_maximum_fusion
  0.8 0.6 broadcast_in_dim.2.embed_ref
  1.4 114.1 %shard_map.118 = bf16[384,640]{1,0:T(8,128)(2,1)} custom-call(bf16[2,384,640]{2,1,0:T(8,128)(2,1)} %kv_ref.1, bf16[384,1280]{1,0:T(8,128)(2,1)} %bitcast.4, bf16[16,320]{1,0:T(8,128)(2,1)} %broadcast_in_dim.2.embed_ref, bf16[320,640]{1,0:T(8,128)(2,1)} %time_ref.1, f32[1280]{0:T(1024)} %gain_one_ref.1, bf16[3,3,1280,640]{3,2,1,0:T(8,128)(2,1)} %conv_ref.1, ...), custom_call_target="tpu_custom_call" | custom-call | flops 13589544960 | bytes 24000000 | tf_op jit(solution)/shard_map/pallas_call | solution.py:674
  115.5 1.9 %copy.15 = bf16[3,128,640]{2,1,0:T(8,128)(2,1)} copy(bf16[3,128,640]{2,1,0:T(8,128)(2,1)} %bitcast.3) | data formatting | bytes 983040

commit v3 on v2

--- a/solution.py
+++ b/solution.py
@@ -503,6 +503,9 @@
         lower = jnp.where(mask, swap(x), 0.0)
         return jnp.concatenate([upper, lower], axis=0).astype(BF16)
 
+    fill = jnp.where(half_mask(1), 1.0, 0.0).astype(BF16)
+    keep = jnp.where(half_mask(1), 0.0, 1.0).astype(BF16)
+
     def run_tasks(couple, unused):
         tasks = []
         for which in range(2):
@@ -514,7 +517,7 @@
         def partial(slot, owner, step):
             rows = pl.ds(pl.multiple_of(lax.rem(owner + step, size) * block, block), block)
             both = kvs[slot, rows, :]
-            return both, jnp.where(left_half, ones, both)
+            return both, both * keep + fill
 
         for which, (slot, owner, query) in enumerate(tasks):
             keys, values = partial(slot, owner, 1)

time: 118 us -> 118 us (level)
  no operation moved by 1% of the time
where the time goes in v3:
time: 118 us; the launch traced here: 117 us
  Pallas kernels  114 us (97%)
  local copies, waits for them, and re-layouts  2.46 us (2%)
    pallas_call x1, Pallas kernels, on_device(): pl.pallas_call(functools.partial(fused_kernel, size), out_shape=jax.Shape...  114 us

profile of v3, /device:TPU:0, one launch (start us, length us, event | category | flops | bytes accessed | tf_op | source)
XLA Modules:
  0.0 117.2 jit_solution(4536074084625602693)
XLA Ops:
  0.7 0.1 sine_convert_fusion
  0.7 0.1 pad_maximum_fusion
  0.8 0.6 broadcast_in_dim.2.embed_ref
  1.4 114.0 %shard_map.118 = bf16[384,640]{1,0:T(8,128)(2,1)} custom-call(bf16[2,384,640]{2,1,0:T(8,128)(2,1)} %kv_ref.1, bf16[384,1280]{1,0:T(8,128)(2,1)} %bitcast.4, bf16[16,320]{1,0:T(8,128)(2,1)} %broadcast_in_dim.2.embed_ref, bf16[320,640]{1,0:T(8,128)(2,1)} %time_ref.1, f32[1280]{0:T(1024)} %gain_one_ref.1, bf16[3,3,1280,640]{3,2,1,0:T(8,128)(2,1)} %conv_ref.1, ...), custom_call_target="tpu_custom_call" | custom-call | flops 13589544960 | bytes 24000000 | tf_op jit(solution)/shard_map/pallas_call | solution.py:677
  115.4 1.9 %copy.15 = bf16[3,128,640]{2,1,0:T(8,128)(2,1)} copy(bf16[3,128,640]{2,1,0:T(8,128)(2,1)} %bitcast.3) | data formatting | bytes 983040
